TPU v7x, 32 devices: a whole 2x2x4 slice. The times are simulated.
32 devices in a mesh: ctx: 8 (over z, x), tp: 4 (over y, core).
Axes of the slice: x: 2, y: 2, z: 4, core: 2. Of those that a mesh axis runs over, the one named last changes fastest.
Arguments:
- pre_gate: bfloat16 [512, 4096], P('ctx', 'tp'), may hold values from -6 to 6
- post_gate: bfloat16 [512, 4096], P('ctx', 'tp'), may hold values from -6 to 6
- features: bfloat16 [512, 4096], P('ctx', 'tp'), may hold values from -6 to 6
- decay_rates: float32 [16, 4096], P(None, 'tp'), may hold values from 0 to 1, as said below
- residues: float32 [16, 4096], P(None, 'tp'), may hold values from -1 to 1
- skip_gain: float32 [4096], P('tp'), may hold values from 0.1 to 1.9
- queries: bfloat16 [512, 4096], P('ctx', 'tp'), may hold values from -20 to 20
- key_rows: bfloat16 [512, 4096], P('ctx', 'tp'), may hold values from -20 to 20
Outputs:
- filtered: bfloat16 [512, 4096], P('ctx', 'tp')
- attended: bfloat16 [512, 4096], P('ctx', 'tp')
Inputs may be any that keep to these rules, and one draw needn't show every extreme that they name: `decay_rates`: positive rates.
All inputs are finite; a program needn't handle non-finite values.
Results may differ from a plain program's by a relative error of at most 0.0065.
Values may be sent and summed in bfloat16 or wider, within the bound.
A program may use at most 128 MiB of HBM per device.

v0:
```python
import jax
import jax.numpy as jnp
from jax import lax
from jax.sharding import PartitionSpec as P

HEAD_SIZE = 128


very_low = -1e30


def shifted_2(x, axis, by):
    peers = lax.axis_size(axis)
    pairs = [(i, i + by) for i in range(peers) if 0 <= i + by < peers]
    return lax.ppermute(x, axis, pairs)


def toeplitz_local(response, driven):
    tok_rows, chan_width = driven.shape
    block_width = min(128, chan_width)
    block_count = chan_width // block_width
    row_index = jnp.arange(tok_rows)
    lag_index = row_index[:, None] - row_index[None, :]
    shift_table = (lag_index[:, :, None] == row_index[None, None, :]).astype(jnp.float32)
    resp_blocks = response.reshape(tok_rows, block_count, block_width).transpose(1, 0, 2)
    drive_blocks = driven.reshape(tok_rows, block_count, block_width).transpose(1, 0, 2)

    def one_block(block_pair):
        resp_block, drive_block = block_pair
        toeplitz = jnp.einsum(
            "tsl,lc->tsc", shift_table, resp_block, precision=lax.Precision.HIGHEST
        )
        return jnp.einsum("tsc,sc->tc", toeplitz, drive_block, precision=lax.Precision.HIGHEST)

    out_blocks = lax.map(one_block, (resp_blocks, drive_blocks))
    return out_blocks.transpose(1, 0, 2).reshape(tok_rows, chan_width)


def on_device(pre_gate, post_gate, features, decay_rates, residues, skip_gain, queries, key_rows):
    tok_rows, chan_width = pre_gate.shape
    product = pre_gate.astype(jnp.float32) * features.astype(jnp.float32)
    driven = lax.optimization_barrier(product.astype(jnp.bfloat16)).astype(jnp.float32)
    offsets = jnp.arange(tok_rows, dtype=jnp.float32)
    powers = jnp.exp(-decay_rates[None, :, :] * offsets[:, None, None])
    response = jnp.einsum("tmc,mc->tc", powers, residues, precision=lax.Precision.HIGHEST)
    local_part = toeplitz_local(response, driven)
    own_state = jnp.einsum("smc,sc->mc", powers[::-1], driven, precision=lax.Precision.HIGHEST)
    block_decay = jnp.exp(-decay_rates * tok_rows)

    def relay_step(turn_index, state_sum):
        return shifted_2(
            (block_decay * state_sum + own_state).astype(jnp.bfloat16), "ctx", 1
        ).astype(jnp.float32)

    incoming = lax.fori_loop(0, lax.axis_size("ctx") - 1, relay_step, jnp.zeros_like(own_state))
    shifted = powers * jnp.exp(-decay_rates)[None, :, :]
    cross_part = jnp.einsum(
        "tmc,mc->tc", shifted, residues * incoming, precision=lax.Precision.HIGHEST
    )
    convolved = local_part + cross_part + skip_gain[None, :] * driven
    filtered = (post_gate.astype(jnp.float32) * convolved).astype(jnp.bfloat16)
    head_count = chan_width // HEAD_SIZE
    scale = HEAD_SIZE ** (-0.5)
    query_heads = queries.reshape(tok_rows, head_count, HEAD_SIZE)
    query_pos = lax.axis_index("ctx") * tok_rows + jnp.arange(tok_rows)
    start_max = jnp.full((head_count, tok_rows), very_low, jnp.float32)
    key_piece = lax.all_gather(key_rows, "ctx", axis=0, tiled=True)
    value_piece = lax.all_gather(filtered, "ctx", axis=0, tiled=True)
    piece_rows = key_piece.shape[0]
    key_heads = key_piece.reshape(piece_rows, head_count, HEAD_SIZE)
    scores = (
        jnp.einsum("qhe,khe->hqk", query_heads, key_heads, preferred_element_type=jnp.float32)
        * scale
    )
    key_pos = jnp.arange(piece_rows)
    allowed = key_pos[None, :] <= query_pos[:, None]
    scores, allowed = (jnp.where(allowed[None], scores, very_low), allowed)
    new_max = jnp.maximum(start_max, jnp.max(scores, axis=-1))
    weights = jnp.where(allowed[None], jnp.exp(scores - new_max[..., None]), 0.0)
    new_sum = jnp.sum(weights, axis=-1)
    piece_rows = value_piece.shape[0]
    value_heads = value_piece.reshape(piece_rows, head_count, HEAD_SIZE)
    new_acc = jnp.einsum(
        "hqk,khe->hqe",
        weights.astype(jnp.bfloat16),
        value_heads,
        preferred_element_type=jnp.float32,
    )
    attended = (
        (new_acc / new_sum[..., None])
        .transpose(1, 0, 2)
        .reshape(tok_rows, chan_width)
        .astype(jnp.bfloat16)
    )
    return (filtered, attended)


def solution(mesh):
    placed = (
        P("ctx", "tp"),
        P("ctx", "tp"),
        P("ctx", "tp"),
        P(None, "tp"),
        P(None, "tp"),
        P("tp"),
        P("ctx", "tp"),
        P("ctx", "tp"),
    )
    return jax.shard_map(
        on_device,
        mesh=mesh,
        in_specs=placed,
        out_specs=(P("ctx", "tp"), P("ctx", "tp")),
        check_vma=False,
    )
```

profile of v0, /device:TPU:0, one launch (start us, length us, event | category | flops | bytes accessed | tf_op | source)
XLA Modules:
  0.0 135.1 jit_solution(7465932337573186422)
XLA Ops:
  8.9 2.5 %multiply_exponential_fusion = f32[64,16,1024]{2,1,0:T(8,128)} fusion(f32[16,1024]{1,0:T(8,128)S(1)} %get-tuple-element.117), kind=kLoop, calls=%fused_computation.16 | loop fusion | flops 1048576 | bytes 4259840 | tf_op jit(solution)/shard_map/exp | solution.py:44
  11.5 2.7 %multiply_reduce_fusion.1 = f32[1024,16]{0,1:T(8,128)S(1)} fusion(f32[64,16,1024]{2,1,0:T(8,128)} %multiply_exponential_fusion, f32[1024,64]{0,1:T(8,128)S(1)} %get-tuple-element.113), kind=kLoop, calls=%fused_computation.14 | loop fusion | flops 2080768 | bytes 4521984 | tf_op jit(solution)/shard_map/smc,sc->mc/dot_general | solution.py:47
  14.1 46.5 %while.23 = (s32[]{:T(128)}, f32[16,1024]{1,0:T(8,128)S(1)}, f32[16,1024]{1,0:T(8,128)S(1)}, f32[16,1024]{1,0:T(8,128)S(1)}, s32[]{:T(128)}, /*index=5*/s32[]{:T(128)}) while((s32[]{:T(128)}, f32[16,1024]{1,0:T(8,128)S(1)}, f32[16,1024]{1,0:T(8,128)S(1)}, f32[16,1024]{1,0:T(8,128)S(1)}, s32[]{:T(128)}, /*index=5*/s32[]{:T(128)}) %tuple.60), condition=%wide.region_3.4_spmd.clone, body=%wide.region_2.3_spmd.clone.sunk | while | flops 81923 | bytes 458871 | solution.py:55
  14.2 4.8 %collective-permute-start = (bf16[16,1024]{1,0:T(8,128)(2,1)S(1)}, bf16[16,1024]{1,0:T(8,128)(2,1)S(1)}, u32[]{:S(2)}, u32[]{:S(2)}) collective-permute-start(bf16[16,1024]{1,0:T(8,128)(2,1)S(1)} %fusion.39), channel_id=1, source_target_pairs={{0,4},{4,8},{8,12},{12,16},{16,20},{20,24},{24,28},{1,5},{5,9},{9,... | collective-permute-start | bytes 98312 | tf_op jit(solution)/shard_map/while/body/eval_jaxpr/ppermute | solution.py:15
  19.0 1.6 %collective-permute-done = bf16[16,1024]{1,0:T(8,128)(2,1)S(1)} collective-permute-done((bf16[16,1024]{1,0:T(8,128)(2,1)S(1)}, bf16[16,1024]{1,0:T(8,128)(2,1)S(1)}, u32[]{:S(2)}, u32[]{:S(2)}) %collective-permute-start) | collective-permute-done | bytes 32800 | tf_op jit(solution)/shard_map/while/body/eval_jaxpr/ppermute | solution.py:15
  20.6 4.2 %collective-permute-start = (bf16[16,1024]{1,0:T(8,128)(2,1)S(1)}, bf16[16,1024]{1,0:T(8,128)(2,1)S(1)}, u32[]{:S(2)}, u32[]{:S(2)}) collective-permute-start(bf16[16,1024]{1,0:T(8,128)(2,1)S(1)} %fusion.39), channel_id=1, source_target_pairs={{0,4},{4,8},{8,12},{12,16},{16,20},{20,24},{24,28},{1,5},{5,9},{9,... | collective-permute-start | bytes 98312 | tf_op jit(solution)/shard_map/while/body/eval_jaxpr/ppermute | solution.py:15
  24.9 1.6 %collective-permute-done = bf16[16,1024]{1,0:T(8,128)(2,1)S(1)} collective-permute-done((bf16[16,1024]{1,0:T(8,128)(2,1)S(1)}, bf16[16,1024]{1,0:T(8,128)(2,1)S(1)}, u32[]{:S(2)}, u32[]{:S(2)}) %collective-permute-start) | collective-permute-done | bytes 32800 | tf_op jit(solution)/shard_map/while/body/eval_jaxpr/ppermute | solution.py:15
  26.5 4.4 %collective-permute-start = (bf16[16,1024]{1,0:T(8,128)(2,1)S(1)}, bf16[16,1024]{1,0:T(8,128)(2,1)S(1)}, u32[]{:S(2)}, u32[]{:S(2)}) collective-permute-start(bf16[16,1024]{1,0:T(8,128)(2,1)S(1)} %fusion.39), channel_id=1, source_target_pairs={{0,4},{4,8},{8,12},{12,16},{16,20},{20,24},{24,28},{1,5},{5,9},{9,... | collective-permute-start | bytes 98312 | tf_op jit(solution)/shard_map/while/body/eval_jaxpr/ppermute | solution.py:15
  32.4 5.3 %collective-permute-start = (bf16[16,1024]{1,0:T(8,128)(2,1)S(1)}, bf16[16,1024]{1,0:T(8,128)(2,1)S(1)}, u32[]{:S(2)}, u32[]{:S(2)}) collective-permute-start(bf16[16,1024]{1,0:T(8,128)(2,1)S(1)} %fusion.39), channel_id=1, source_target_pairs={{0,4},{4,8},{8,12},{12,16},{16,20},{20,24},{24,28},{1,5},{5,9},{9,... | collective-permute-start | bytes 98312 | tf_op jit(solution)/shard_map/while/body/eval_jaxpr/ppermute | solution.py:15
  37.7 1.9 %collective-permute-done = bf16[16,1024]{1,0:T(8,128)(2,1)S(1)} collective-permute-done((bf16[16,1024]{1,0:T(8,128)(2,1)S(1)}, bf16[16,1024]{1,0:T(8,128)(2,1)S(1)}, u32[]{:S(2)}, u32[]{:S(2)}) %collective-permute-start) | collective-permute-done | bytes 32800 | tf_op jit(solution)/shard_map/while/body/eval_jaxpr/ppermute | solution.py:15
  39.6 5.0 %collective-permute-start = (bf16[16,1024]{1,0:T(8,128)(2,1)S(1)}, bf16[16,1024]{1,0:T(8,128)(2,1)S(1)}, u32[]{:S(2)}, u32[]{:S(2)}) collective-permute-start(bf16[16,1024]{1,0:T(8,128)(2,1)S(1)} %fusion.39), channel_id=1, source_target_pairs={{0,4},{4,8},{8,12},{12,16},{16,20},{20,24},{24,28},{1,5},{5,9},{9,... | collective-permute-start | bytes 98312 | tf_op jit(solution)/shard_map/while/body/eval_jaxpr/ppermute | solution.py:15
  46.2 5.9 %collective-permute-start = (bf16[16,1024]{1,0:T(8,128)(2,1)S(1)}, bf16[16,1024]{1,0:T(8,128)(2,1)S(1)}, u32[]{:S(2)}, u32[]{:S(2)}) collective-permute-start(bf16[16,1024]{1,0:T(8,128)(2,1)S(1)} %fusion.39), channel_id=1, source_target_pairs={{0,4},{4,8},{8,12},{12,16},{16,20},{20,24},{24,28},{1,5},{5,9},{9,... | collective-permute-start | bytes 98312 | tf_op jit(solution)/shard_map/while/body/eval_jaxpr/ppermute | solution.py:15
  53.7 5.3 %collective-permute-start = (bf16[16,1024]{1,0:T(8,128)(2,1)S(1)}, bf16[16,1024]{1,0:T(8,128)(2,1)S(1)}, u32[]{:S(2)}, u32[]{:S(2)}) collective-permute-start(bf16[16,1024]{1,0:T(8,128)(2,1)S(1)} %fusion.39), channel_id=1, source_target_pairs={{0,4},{4,8},{8,12},{12,16},{16,20},{20,24},{24,28},{1,5},{5,9},{9,... | collective-permute-start | bytes 98312 | tf_op jit(solution)/shard_map/while/body/eval_jaxpr/ppermute | solution.py:15
  60.6 2.0 %multiply_reduce_fusion = (f32[1024,64]{0,1:T(8,128)S(1)}, f32[1024,64]{0,1:T(8,128)S(1)}) fusion(f32[1024,16]{0,1:T(8,128)S(1)} %multiply_bitcast_fusion, f32[16,1024]{1,0:T(8,128)S(1)} %get-tuple-element.115, f32[16,1024]{1,0:T(8,128)S(1)} %get-tuple-element.117, f32[1024,16]{0,1:T(8,128)S(1)} %bitcast.99), kind=kLoop, calls=%fused_computation.13 | loop fusion | flops 6160384 | bytes 786432 | tf_op jit(solution)/shard_map/tmc,mc->tc/dot_general | solution.py:57
  62.8 17.7 %while.22 = (s32[]{:T(128)}, f32[8,64,128]{2,1,0:T(8,128)S(1)}, f32[8,64,128]{2,1,0:T(8,128)S(1)}, f32[8,64,128]{2,0,1:T(8,128)S(1)}, s32[64,64]{1,0:T(8,128)S(1)}, /*index=5*/s32[]{:T(128)}) while((s32[]{:T(128)}, f32[8,64,128]{2,1,0:T(8,128)S(1)}, f32[8,64,128]{2,1,0:T(8,128)S(1)}, f32[8,64,128]{2,0,1:T(8,128)S(1)}, ...), condition=%wide.region_1.2_spmd.clone, body=%wide.region_0.1_spmd.clone.sunk | while | flops 404217856 | bytes 311377 | solution.py:35
  62.9 2.1 %fusion.38 = f32[128,64]{0,1:T(8,128)S(1)} fusion(f32[64,128,1]{1,0,2:T(8,128)S(1)} %bitcast.94, f32[128,64]{0,1:T(8,128)S(1)} %dynamic-slice_bitcast_fusion.2, s32[64,64]{1,0:T(8,128)S(1)} %get-tuple-element.210), kind=kOutput, calls=%fused_computation.5.clone.1 | convolution fusion | flops 404217856 | bytes 114688 | tf_op jit(solution)/shard_map/while/body/eval_jaxpr/tsl,lc->tsc/dot_general | solution.py:30
  65.1 2.1 %fusion.38 = f32[128,64]{0,1:T(8,128)S(1)} fusion(f32[64,128,1]{1,0,2:T(8,128)S(1)} %bitcast.94, f32[128,64]{0,1:T(8,128)S(1)} %dynamic-slice_bitcast_fusion.2, s32[64,64]{1,0:T(8,128)S(1)} %get-tuple-element.210), kind=kOutput, calls=%fused_computation.5.clone.1 | convolution fusion | flops 404217856 | bytes 114688 | tf_op jit(solution)/shard_map/while/body/eval_jaxpr/tsl,lc->tsc/dot_general | solution.py:30
  67.3 2.1 %fusion.38 = f32[128,64]{0,1:T(8,128)S(1)} fusion(f32[64,128,1]{1,0,2:T(8,128)S(1)} %bitcast.94, f32[128,64]{0,1:T(8,128)S(1)} %dynamic-slice_bitcast_fusion.2, s32[64,64]{1,0:T(8,128)S(1)} %get-tuple-element.210), kind=kOutput, calls=%fused_computation.5.clone.1 | convolution fusion | flops 404217856 | bytes 114688 | tf_op jit(solution)/shard_map/while/body/eval_jaxpr/tsl,lc->tsc/dot_general | solution.py:30
  69.5 2.1 %fusion.38 = f32[128,64]{0,1:T(8,128)S(1)} fusion(f32[64,128,1]{1,0,2:T(8,128)S(1)} %bitcast.94, f32[128,64]{0,1:T(8,128)S(1)} %dynamic-slice_bitcast_fusion.2, s32[64,64]{1,0:T(8,128)S(1)} %get-tuple-element.210), kind=kOutput, calls=%fused_computation.5.clone.1 | convolution fusion | flops 404217856 | bytes 114688 | tf_op jit(solution)/shard_map/while/body/eval_jaxpr/tsl,lc->tsc/dot_general | solution.py:30
  71.7 2.1 %fusion.38 = f32[128,64]{0,1:T(8,128)S(1)} fusion(f32[64,128,1]{1,0,2:T(8,128)S(1)} %bitcast.94, f32[128,64]{0,1:T(8,128)S(1)} %dynamic-slice_bitcast_fusion.2, s32[64,64]{1,0:T(8,128)S(1)} %get-tuple-element.210), kind=kOutput, calls=%fused_computation.5.clone.1 | convolution fusion | flops 404217856 | bytes 114688 | tf_op jit(solution)/shard_map/while/body/eval_jaxpr/tsl,lc->tsc/dot_general | solution.py:30
  73.9 2.1 %fusion.38 = f32[128,64]{0,1:T(8,128)S(1)} fusion(f32[64,128,1]{1,0,2:T(8,128)S(1)} %bitcast.94, f32[128,64]{0,1:T(8,128)S(1)} %dynamic-slice_bitcast_fusion.2, s32[64,64]{1,0:T(8,128)S(1)} %get-tuple-element.210), kind=kOutput, calls=%fused_computation.5.clone.1 | convolution fusion | flops 404217856 | bytes 114688 | tf_op jit(solution)/shard_map/while/body/eval_jaxpr/tsl,lc->tsc/dot_general | solution.py:30
  76.1 2.1 %fusion.38 = f32[128,64]{0,1:T(8,128)S(1)} fusion(f32[64,128,1]{1,0,2:T(8,128)S(1)} %bitcast.94, f32[128,64]{0,1:T(8,128)S(1)} %dynamic-slice_bitcast_fusion.2, s32[64,64]{1,0:T(8,128)S(1)} %get-tuple-element.210), kind=kOutput, calls=%fused_computation.5.clone.1 | convolution fusion | flops 404217856 | bytes 114688 | tf_op jit(solution)/shard_map/while/body/eval_jaxpr/tsl,lc->tsc/dot_general | solution.py:30
  78.3 2.1 %fusion.38 = f32[128,64]{0,1:T(8,128)S(1)} fusion(f32[64,128,1]{1,0,2:T(8,128)S(1)} %bitcast.94, f32[128,64]{0,1:T(8,128)S(1)} %dynamic-slice_bitcast_fusion.2, s32[64,64]{1,0:T(8,128)S(1)} %get-tuple-element.210), kind=kOutput, calls=%fused_computation.5.clone.1 | convolution fusion | flops 404217856 | bytes 114688 | tf_op jit(solution)/shard_map/while/body/eval_jaxpr/tsl,lc->tsc/dot_general | solution.py:30
  83.6 41.9 %all-gather.5.cloned.1.call-done = bf16[512,1024]{1,0:T(8,128)(2,1)} async-done(((bf16[64,1024]{1,0:T(8,128)(2,1)}), bf16[512,1024]{1,0:T(8,128)(2,1)}) %all-gather.5.cloned.1.call-update) | async-done | bytes 1048592 | tf_op jit(solution)/shard_map/all_gather | solution.py:68
  (78 shorter events, 14.5 us)
Async XLA Ops:
  7.2 75.7 %copy-start = (bf16[64,1024]{1,0:T(8,128)(2,1)S(1)}, bf16[64,1024]{1,0:T(8,128)(2,1)}, u32[]{:S(2)}) copy-start(bf16[64,1024]{1,0:T(8,128)(2,1)} %param.18) | copy-start | bytes 393220
  7.2 4.2 %copy-start.2 = (bf16[64,1024]{1,0:T(8,128)(2,1)S(1)}, bf16[64,1024]{1,0:T(8,128)(2,1)}, u32[]{:S(2)}) copy-start(bf16[64,1024]{1,0:T(8,128)(2,1)} %param.12) | copy-start | bytes 393220
  7.2 4.2 %copy-start.1 = (bf16[64,1024]{1,0:T(8,128)(2,1)S(1)}, bf16[64,1024]{1,0:T(8,128)(2,1)}, u32[]{:S(2)}) copy-start(bf16[64,1024]{1,0:T(8,128)(2,1)} %param.14) | copy-start | bytes 393220
  7.2 74.1 %all-gather.3.cloned.1.call-start = ((), (), s32[]{:S(2)}) async-start(), calls=%async_computation | async-start | bytes 1179648 | tf_op jit(solution)/shard_map/all_gather | solution.py:67
  7.9 117.6 %all-gather.5.cloned.1.call-start = ((), (), s32[]{:S(2)}) async-start(), calls=%async_computation.1 | async-start | bytes 1179648 | tf_op jit(solution)/shard_map/all_gather | solution.py:68
  11.4 49.2 %copy-start.4 = (f32[16,1024]{1,0:T(8,128)S(1)}, f32[16,1024]{1,0:T(8,128)}, u32[]{:S(2)}) copy-start(f32[16,1024]{1,0:T(8,128)} %param.16) | copy-start | bytes 196612
  14.2 6.4 %collective-permute-start = (bf16[16,1024]{1,0:T(8,128)(2,1)S(1)}, bf16[16,1024]{1,0:T(8,128)(2,1)S(1)}, u32[]{:S(2)}, u32[]{:S(2)}) collective-permute-start(bf16[16,1024]{1,0:T(8,128)(2,1)S(1)} %fusion.39), channel_id=1, source_target_pairs={{0,4},{4,8},{8,12},{12,16},{16,20},{20,24},{24,28},{1,5},{5,9},{9,... | collective-permute-start | bytes 98312 | tf_op jit(solution)/shard_map/while/body/eval_jaxpr/ppermute | solution.py:15
  20.6 5.8 %collective-permute-start = (bf16[16,1024]{1,0:T(8,128)(2,1)S(1)}, bf16[16,1024]{1,0:T(8,128)(2,1)S(1)}, u32[]{:S(2)}, u32[]{:S(2)}) collective-permute-start(bf16[16,1024]{1,0:T(8,128)(2,1)S(1)} %fusion.39), channel_id=1, source_target_pairs={{0,4},{4,8},{8,12},{12,16},{16,20},{20,24},{24,28},{1,5},{5,9},{9,... | collective-permute-start | bytes 98312 | tf_op jit(solution)/shard_map/while/body/eval_jaxpr/ppermute | solution.py:15
  26.5 5.9 %collective-permute-start = (bf16[16,1024]{1,0:T(8,128)(2,1)S(1)}, bf16[16,1024]{1,0:T(8,128)(2,1)S(1)}, u32[]{:S(2)}, u32[]{:S(2)}) collective-permute-start(bf16[16,1024]{1,0:T(8,128)(2,1)S(1)} %fusion.39), channel_id=1, source_target_pairs={{0,4},{4,8},{8,12},{12,16},{16,20},{20,24},{24,28},{1,5},{5,9},{9,... | collective-permute-start | bytes 98312 | tf_op jit(solution)/shard_map/while/body/eval_jaxpr/ppermute | solution.py:15
  32.4 7.1 %collective-permute-start = (bf16[16,1024]{1,0:T(8,128)(2,1)S(1)}, bf16[16,1024]{1,0:T(8,128)(2,1)S(1)}, u32[]{:S(2)}, u32[]{:S(2)}) collective-permute-start(bf16[16,1024]{1,0:T(8,128)(2,1)S(1)} %fusion.39), channel_id=1, source_target_pairs={{0,4},{4,8},{8,12},{12,16},{16,20},{20,24},{24,28},{1,5},{5,9},{9,... | collective-permute-start | bytes 98312 | tf_op jit(solution)/shard_map/while/body/eval_jaxpr/ppermute | solution.py:15
  39.6 6.6 %collective-permute-start = (bf16[16,1024]{1,0:T(8,128)(2,1)S(1)}, bf16[16,1024]{1,0:T(8,128)(2,1)S(1)}, u32[]{:S(2)}, u32[]{:S(2)}) collective-permute-start(bf16[16,1024]{1,0:T(8,128)(2,1)S(1)} %fusion.39), channel_id=1, source_target_pairs={{0,4},{4,8},{8,12},{12,16},{16,20},{20,24},{24,28},{1,5},{5,9},{9,... | collective-permute-start | bytes 98312 | tf_op jit(solution)/shard_map/while/body/eval_jaxpr/ppermute | solution.py:15
  46.2 7.5 %collective-permute-start = (bf16[16,1024]{1,0:T(8,128)(2,1)S(1)}, bf16[16,1024]{1,0:T(8,128)(2,1)S(1)}, u32[]{:S(2)}, u32[]{:S(2)}) collective-permute-start(bf16[16,1024]{1,0:T(8,128)(2,1)S(1)} %fusion.39), channel_id=1, source_target_pairs={{0,4},{4,8},{8,12},{12,16},{16,20},{20,24},{24,28},{1,5},{5,9},{9,... | collective-permute-start | bytes 98312 | tf_op jit(solution)/shard_map/while/body/eval_jaxpr/ppermute | solution.py:15
  53.7 6.9 %collective-permute-start = (bf16[16,1024]{1,0:T(8,128)(2,1)S(1)}, bf16[16,1024]{1,0:T(8,128)(2,1)S(1)}, u32[]{:S(2)}, u32[]{:S(2)}) collective-permute-start(bf16[16,1024]{1,0:T(8,128)(2,1)S(1)} %fusion.39), channel_id=1, source_target_pairs={{0,4},{4,8},{8,12},{12,16},{16,20},{20,24},{24,28},{1,5},{5,9},{9,... | collective-permute-start | bytes 98312 | tf_op jit(solution)/shard_map/while/body/eval_jaxpr/ppermute | solution.py:15
  62.8 17.7 %copy-start.3 = (bf16[64,1024]{1,0:T(8,128)(2,1)S(1)}, bf16[64,1024]{1,0:T(8,128)(2,1)}, u32[]{:S(2)}) copy-start(bf16[64,1024]{1,0:T(8,128)(2,1)} %param.13) | copy-start | bytes 393220
  62.8 17.7 %copy-start.5 = (f32[1024]{0:T(1024)S(1)}, f32[1024]{0:T(1024)}, u32[]{:S(2)}) copy-start(f32[1024]{0:T(1024)} %param.17) | copy-start | bytes 12292
Sparse Core Ops, SparseCore 0:
  10.2 43.6 all-gather.2
  81.3 44.1 all-gather.4
where the time goes:
time: 135 us
  waiting for transfers between devices  53.9 us (40%)
  starting transfers between devices  35 us (26%)
  matrix products  17.8 us (13%)
  between operations  14.2 us (11%)
  other arithmetic  9.48 us (7%)
  local copies, waits for them, and re-layouts  4.16 us (3%)
    all_gather x1, waiting for transfers between devices, on_device(): value_piece = lax.all_gather(filtered, 'ctx', axis=0, tiled=True)  41.9 us
    ppermute x7, starting transfers between devices, shifted_2(): return lax.ppermute(x, axis, pairs)  34.9 us
    dot_general x8, matrix products, one_block(): jnp.einsum('tsl,lc->tsc', shift_table, resp_block, precision=lax.Precisio...  16.9 us
    ppermute x7, waiting for transfers between devices, shifted_2(): return lax.ppermute(x, axis, pairs)  11.3 us
  transfers between devices with their start and end apart: 9, of which 8 were waited for; matrix products, arithmetic and copies ran while one was open for 21% of the time, Pallas kernels for 0%

commit v1 on v0

--- a/solution.py
+++ b/solution.py
@@ -1,6 +1,8 @@
 import jax
 import jax.numpy as jnp
 from jax import lax
+from jax.experimental import pallas as pl
+from jax.experimental.pallas import tpu as pltpu
 from jax.sharding import PartitionSpec as P
 
 HEAD_SIZE = 128
@@ -95,6 +97,196 @@
     return (filtered, attended)
 
 
+MESH = pl.DeviceIdType.MESH
+QK, STATE, PREFIX, VALUE, OUT = range(5)
+
+
+def mixer_kernel(
+    pre_ref, post_ref, feat_ref, decay_ref, resid_ref, skip_ref, q_ref, k_ref,
+    filt_ref, att_ref,
+    qk_send, qk_all, st_send, st_all, pf_send, pf_all, v_send, v_all, att_send, att_all,
+    driven, conv, factor, gain, state, jump, weights, totals,
+    send_sems, recv_sems,
+):
+    heads, rows, size = v_send.shape
+    modes = decay_ref.shape[0]
+    me = lax.axis_index("ctx")
+
+    barrier = pltpu.get_barrier_semaphore()
+    for d in range(1, heads):
+        pl.semaphore_signal(
+            barrier, inc=1, device_id={"ctx": lax.rem(me + d, heads)}, device_id_type=MESH
+        )
+
+    def exchange(phase, src, dst):
+        copies = []
+        for d in range(1, heads):
+            peer = lax.rem(me + d, heads)
+            copy = pltpu.make_async_remote_copy(
+                src_ref=src.at[peer],
+                dst_ref=dst.at[me],
+                send_sem=send_sems.at[phase, d],
+                recv_sem=recv_sems.at[phase, d],
+                device_id={"ctx": peer},
+                device_id_type=MESH,
+            )
+            copy.start()
+            copies.append(copy)
+        dst[me] = src[me]
+        return copies
+
+    for h in range(heads):
+        lanes = slice(h * size, (h + 1) * size)
+        product = pre_ref[:, lanes].astype(jnp.float32) * feat_ref[:, lanes].astype(jnp.float32)
+        driven[h * rows:(h + 1) * rows] = product.astype(jnp.bfloat16).astype(jnp.float32)
+        decay = decay_ref[:, lanes]
+        factor[h * modes:(h + 1) * modes] = jnp.exp(-decay)
+        jump[h * modes:(h + 1) * modes] = jnp.exp(-decay * rows)
+        gain[h * modes:(h + 1) * modes] = resid_ref[:, lanes]
+
+    def by_mode(ref):
+        return [ref[pl.ds(m, heads, stride=modes), :] for m in range(modes)]
+
+    f = by_mode(factor)
+    step = 8
+
+    def end_state(turn, s):
+        for u in range(step):
+            d = driven[pl.ds(turn * step + u, heads, stride=rows), :]
+            s = [f[m] * s[m] + d for m in range(modes)]
+        return s
+
+    zero = [jnp.zeros((heads, size), jnp.float32)] * modes
+    ended = lax.fori_loop(0, rows // step, end_state, zero)
+    for m in range(modes):
+        state[pl.ds(m, heads, stride=modes), :] = ended[m]
+    for h in range(heads):
+        st_send[h] = state[h * modes:(h + 1) * modes].astype(jnp.bfloat16)
+
+    pl.semaphore_wait(barrier, heads - 1)
+    st_copies = exchange(STATE, st_send, st_all)
+    for h in range(heads):
+        lanes = slice(h * size, (h + 1) * size)
+        qk_send[h, 0] = q_ref[:, lanes]
+        qk_send[h, 1] = k_ref[:, lanes]
+    qk_copies = exchange(QK, qk_send, qk_all)
+
+    for copy in st_copies:
+        copy.wait_recv()
+    leap = jump[pl.ds(pl.multiple_of(me * modes, modes), modes), :]
+    running = jnp.zeros((modes, size), jnp.float32)
+    for c in range(heads):
+        pf_send[c] = running.astype(jnp.bfloat16)
+        running = leap * running + st_all[c].astype(jnp.float32)
+    pf_copies = exchange(PREFIX, pf_send, pf_all)
+    for copy in pf_copies:
+        copy.wait_recv()
+    for h in range(heads):
+        state[h * modes:(h + 1) * modes] = pf_all[h].astype(jnp.float32)
+
+    g = by_mode(gain)
+    skip = skip_ref[...]
+
+    def filter_rows(turn, s):
+        for u in range(step):
+            at = pl.ds(turn * step + u, heads, stride=rows)
+            d = driven[at, :]
+            s = [f[m] * s[m] + d for m in range(modes)]
+            terms = [g[m] * s[m] for m in range(modes)] + [skip * d]
+            while len(terms) > 1:
+                terms = [sum(terms[i + 1:i + 2], terms[i]) for i in range(0, len(terms), 2)]
+            conv[at, :] = terms[0]
+        return s
+
+    lax.fori_loop(0, rows // step, filter_rows, by_mode(state))
+    for h in range(heads):
+        lanes = slice(h * size, (h + 1) * size)
+        gated = post_ref[:, lanes].astype(jnp.float32) * conv[h * rows:(h + 1) * rows]
+        gated = gated.astype(jnp.bfloat16)
+        filt_ref[:, lanes] = gated
+        v_send[h] = gated
+    v_copies = exchange(VALUE, v_send, v_all)
+
+    for copy in qk_copies:
+        copy.wait_recv()
+    pair = 2
+    tall = pair * rows
+    scale = size ** -0.5
+    blocks = heads // pair
+    for b in range(blocks):
+        wide = (b + 1) * tall
+        q = qk_all[b * pair:(b + 1) * pair, 0].reshape(tall, size)
+        k = qk_all[0:(b + 1) * pair, 1].reshape(wide, size)
+        score = lax.dot_general(
+            q, k, (((1,), (1,)), ((), ())), preferred_element_type=jnp.float32
+        ) * scale
+        row = lax.broadcasted_iota(jnp.int32, (tall, wide), 0) + b * tall
+        column = lax.broadcasted_iota(jnp.int32, (tall, wide), 1)
+        score = jnp.where(column <= row, score, very_low)
+        weight = jnp.exp(score - jnp.max(score, axis=1, keepdims=True))
+        totals[b * tall:(b + 1) * tall] = jnp.broadcast_to(
+            jnp.sum(weight, axis=1, keepdims=True), (tall, size)
+        )
+        weights[b * tall:(b + 1) * tall, 0:wide] = weight.astype(jnp.bfloat16)
+
+    for copy in v_copies:
+        copy.wait_recv()
+    for b in range(blocks):
+        wide = (b + 1) * tall
+        v = v_all[0:(b + 1) * pair].reshape(wide, size)
+        acc = jnp.dot(
+            weights[b * tall:(b + 1) * tall, 0:wide], v, preferred_element_type=jnp.float32
+        )
+        out = (acc / totals[b * tall:(b + 1) * tall]).astype(jnp.bfloat16)
+        att_send[b * pair:(b + 1) * pair] = out.reshape(pair, rows, size)
+    att_copies = exchange(OUT, att_send, att_all)
+    for copy in att_copies:
+        copy.wait_recv()
+    for h in range(heads):
+        att_ref[:, h * size:(h + 1) * size] = att_all[h]
+    for copy in st_copies + qk_copies + pf_copies + v_copies + att_copies:
+        copy.wait_send()
+
+
+def by_heads(pre_gate, post_gate, features, decay_rates, residues, skip_gain, queries, key_rows):
+    rows, width = pre_gate.shape
+    modes = decay_rates.shape[0]
+    size = HEAD_SIZE
+    heads = width // size
+    shape = jax.ShapeDtypeStruct((rows, width), jnp.bfloat16)
+    bf16 = lambda *dims: pltpu.VMEM(dims, jnp.bfloat16)
+    f32 = lambda *dims: pltpu.VMEM(dims, jnp.float32)
+    small = [bf16(heads, modes, size)] * 4
+    blocks = [bf16(heads, rows, size)] * 4
+    return tuple(pl.pallas_call(
+        mixer_kernel,
+        out_shape=(shape, shape),
+        in_specs=[pl.BlockSpec(memory_space=pltpu.VMEM)] * 8,
+        out_specs=(pl.BlockSpec(memory_space=pltpu.VMEM),) * 2,
+        scratch_shapes=[
+            bf16(heads, 2, rows, size), bf16(heads, 2, rows, size),
+            *small, *blocks,
+            f32(heads * rows, size), f32(heads * rows, size),
+            *[f32(heads * modes, size)] * 4,
+            bf16(heads * rows, heads * rows), f32(heads * rows, size),
+            pltpu.SemaphoreType.DMA((5, heads)),
+            pltpu.SemaphoreType.DMA((5, heads)),
+        ],
+        compiler_params=pltpu.CompilerParams(
+            collective_id=0, has_side_effects=True, vmem_limit_bytes=32 * 1024 * 1024
+        ),
+    )(
+        pre_gate, post_gate, features, decay_rates, residues,
+        skip_gain.reshape(heads, size), queries, key_rows,
+    ))
+
+
+def pick_body(*args):
+    rows, width = args[0].shape
+    whole_heads = lax.axis_size("ctx") * HEAD_SIZE == width
+    return (by_heads if whole_heads and rows % 16 == 0 else on_device)(*args)
+
+
 def solution(mesh):
     placed = (
         P("ctx", "tp"),
@@ -107,7 +299,7 @@
         P("ctx", "tp"),
     )
     return jax.shard_map(
-        on_device,
+        pick_body,
         mesh=mesh,
         in_specs=placed,
         out_specs=(P("ctx", "tp"), P("ctx", "tp")),

time: 135 us -> 34.6 us (0.26)
  waiting for transfers between devices: 53.9 us -> 0 us
  starting transfers between devices: 35 us -> 0 us
  Pallas kernels: 0 us -> 25.4 us
  matrix products: 17.8 us -> 0 us
  between operations: 14.2 us -> 0.66 us
  other arithmetic: 9.48 us -> 0 us
  local copies, waits for them, and re-layouts: 4.16 us -> 8.19 us
    all_gather x2 -> x0, waiting for transfers between devices: 41.9 us -> none  [the longest x1 41.9 us: on_device(): value_piece = lax.all_gather(filtered, 'ctx', axis=0, tiled=True)]
    ppermute x7 -> x0, starting transfers between devices: 34.9 us -> none  [shifted_2(): return lax.ppermute(x, axis, pairs)]
    pallas_call x0 -> x1, Pallas kernels: none -> 25.4 us  [by_heads(): pl.pallas_call(mixer_kernel, out_shape=(shape, shape), in_specs=[pl.Block...]
    dot_general x10 -> x0, matrix products: 17.8 us -> none  [the longest x8 16.9 us: one_block(): jnp.einsum('tsl,lc->tsc', shift_table, resp_block, precision=lax.Precisio...]
    ppermute x7 -> x0, waiting for transfers between devices: 11.3 us -> none  [shifted_2(): return lax.ppermute(x, axis, pairs)]
    unnamed x13 -> x18, local copies, waits for them, and re-layouts: 0.08 us -> 8.19 us
    dot_general x2 -> x0, other arithmetic: 4.71 us -> none  [the longest x1 2.67 us: on_device(): jnp.einsum('smc,sc->mc', powers[::-1], driven, precision=lax.Precision.HI...]
    exp x2 -> x0, other arithmetic: 3.35 us -> none  [the longest x1 2.48 us: on_device(): powers = jnp.exp(-decay_rates[None, :, :] * offsets[:, None, None])]
  transfers between devices with their start and end apart: 9 -> 0, of which waited for: 8 -> 0; matrix products, arithmetic and copies ran while one was open for 21% -> 0% of each run, Pallas kernels for 0% -> 0%
where the time goes in v1:
time: 34.6 us; the launch traced here: 34.2 us
  Pallas kernels  25.4 us (73%)
  local copies, waits for them, and re-layouts  8.19 us (24%)
  between operations  0.66 us (2%)
    pallas_call x1, Pallas kernels, by_heads(): pl.pallas_call(mixer_kernel, out_shape=(shape, shape), in_specs=[pl.Block...  25.4 us
    unnamed x18, local copies, waits for them, and re-layouts  8.19 us

profile of v1, /device:TPU:0, one launch (start us, length us, event | category | flops | bytes accessed | tf_op | source)
XLA Modules:
  0.0 34.2 jit_solution(9746622521452864048)
XLA Ops:
  0.6 0.0 copy-start
  0.6 0.9 %copy-done = bf16[64,1024]{1,0:T(8,128)(2,1)S(1)} copy-done((bf16[64,1024]{1,0:T(8,128)(2,1)S(1)}, bf16[64,1024]{1,0:T(8,128)(2,1)}, u32[]{:S(2)}) %copy-start) | copy-done | bytes 131096
  1.5 0.0 copy-start.1
  1.5 0.9 %copy-done.1 = bf16[64,1024]{1,0:T(8,128)(2,1)S(1)} copy-done((bf16[64,1024]{1,0:T(8,128)(2,1)S(1)}, bf16[64,1024]{1,0:T(8,128)(2,1)}, u32[]{:S(2)}) %copy-start.1) | copy-done | bytes 131096
  2.4 0.0 copy-start.2
  2.4 0.9 %copy-done.2 = bf16[64,1024]{1,0:T(8,128)(2,1)S(1)} copy-done((bf16[64,1024]{1,0:T(8,128)(2,1)S(1)}, bf16[64,1024]{1,0:T(8,128)(2,1)}, u32[]{:S(2)}) %copy-start.2) | copy-done | bytes 131096
  3.3 0.0 copy-start.3
  3.3 0.9 %copy-done.3 = bf16[64,1024]{1,0:T(8,128)(2,1)S(1)} copy-done((bf16[64,1024]{1,0:T(8,128)(2,1)S(1)}, bf16[64,1024]{1,0:T(8,128)(2,1)}, u32[]{:S(2)}) %copy-start.3) | copy-done | bytes 131096
  4.3 0.0 copy-start.4
  4.3 0.9 %copy-done.4 = bf16[64,1024]{1,0:T(8,128)(2,1)S(1)} copy-done((bf16[64,1024]{1,0:T(8,128)(2,1)S(1)}, bf16[64,1024]{1,0:T(8,128)(2,1)}, u32[]{:S(2)}) %copy-start.4) | copy-done | bytes 131096
  5.2 0.0 copy-start.5
  5.2 0.8 %copy-done.5 = f32[16,1024]{1,0:T(8,128)S(1)} copy-done((f32[16,1024]{1,0:T(8,128)S(1)}, f32[16,1024]{1,0:T(8,128)}, u32[]{:S(2)}) %copy-start.5) | copy-done | bytes 65560
  6.0 0.0 copy-start.6
  6.0 0.8 %copy-done.6 = f32[16,1024]{1,0:T(8,128)S(1)} copy-done((f32[16,1024]{1,0:T(8,128)S(1)}, f32[16,1024]{1,0:T(8,128)}, u32[]{:S(2)}) %copy-start.6) | copy-done | bytes 65560
  6.8 0.0 copy-start.7
  6.8 0.7 %copy-done.7 = f32[1024]{0:T(1024)S(1)} copy-done((f32[1024]{0:T(1024)S(1)}, f32[1024]{0:T(1024)}, u32[]{:S(2)}) %copy-start.7) | copy-done | bytes 4120
  7.5 25.4 %shard_map.95 = (bf16[64,1024]{1,0:T(8,128)(2,1)S(1)}, bf16[64,1024]{1,0:T(8,128)(2,1)S(1)}) custom-call(bf16[64,1024]{1,0:T(8,128)(2,1)S(1)} %copy-done, bf16[64,1024]{1,0:T(8,128)(2,1)S(1)} %copy-done.1, bf16[64,1024]{1,0:T(8,128)(2,1)S(1)} %copy-done.2, f32[16,1024]{1,0:T(8,128)S(1)} %copy-done.5, f32[16,1024]{1,0:T(8,128)S(1)} %copy-done.6, ...), custom_call_target="tpu_custom_call" | custom-call | tf_op jit(solution)/shard_map/pallas_call | solution.py:261
  32.9 0.7 %copy.12 = bf16[64,1024]{1,0:T(8,128)(2,1)} copy(bf16[64,1024]{1,0:T(8,128)(2,1)S(1)} %get-tuple-element.4) | data formatting | bytes 262144
  33.6 0.7 %copy.13 = bf16[64,1024]{1,0:T(8,128)(2,1)} copy(bf16[64,1024]{1,0:T(8,128)(2,1)S(1)} %get-tuple-element.5) | data formatting | bytes 262144
Async XLA Ops:
  0.6 0.9 %copy-start = (bf16[64,1024]{1,0:T(8,128)(2,1)S(1)}, bf16[64,1024]{1,0:T(8,128)(2,1)}, u32[]{:S(2)}) copy-start(bf16[64,1024]{1,0:T(8,128)(2,1)} %pre_ref.1) | copy-start | bytes 393220
  1.5 0.9 %copy-start.1 = (bf16[64,1024]{1,0:T(8,128)(2,1)S(1)}, bf16[64,1024]{1,0:T(8,128)(2,1)}, u32[]{:S(2)}) copy-start(bf16[64,1024]{1,0:T(8,128)(2,1)} %post_ref.1) | copy-start | bytes 393220
  2.4 0.9 %copy-start.2 = (bf16[64,1024]{1,0:T(8,128)(2,1)S(1)}, bf16[64,1024]{1,0:T(8,128)(2,1)}, u32[]{:S(2)}) copy-start(bf16[64,1024]{1,0:T(8,128)(2,1)} %feat_ref.1) | copy-start | bytes 393220
  3.3 0.9 %copy-start.3 = (bf16[64,1024]{1,0:T(8,128)(2,1)S(1)}, bf16[64,1024]{1,0:T(8,128)(2,1)}, u32[]{:S(2)}) copy-start(bf16[64,1024]{1,0:T(8,128)(2,1)} %q_ref.1) | copy-start | bytes 393220
  4.3 0.9 %copy-start.4 = (bf16[64,1024]{1,0:T(8,128)(2,1)S(1)}, bf16[64,1024]{1,0:T(8,128)(2,1)}, u32[]{:S(2)}) copy-start(bf16[64,1024]{1,0:T(8,128)(2,1)} %k_ref.1) | copy-start | bytes 393220
  5.2 0.8 %copy-start.5 = (f32[16,1024]{1,0:T(8,128)S(1)}, f32[16,1024]{1,0:T(8,128)}, u32[]{:S(2)}) copy-start(f32[16,1024]{1,0:T(8,128)} %decay_ref.1) | copy-start | bytes 196612
  6.0 0.8 %copy-start.6 = (f32[16,1024]{1,0:T(8,128)S(1)}, f32[16,1024]{1,0:T(8,128)}, u32[]{:S(2)}) copy-start(f32[16,1024]{1,0:T(8,128)} %resid_ref.1) | copy-start | bytes 196612
  6.8 0.7 %copy-start.7 = (f32[1024]{0:T(1024)S(1)}, f32[1024]{0:T(1024)}, u32[]{:S(2)}) copy-start(f32[1024]{0:T(1024)} %param.13) | copy-start | bytes 12292

commit v2 on v1

--- a/solution.py
+++ b/solution.py
@@ -101,13 +101,28 @@
 QK, STATE, PREFIX, VALUE, OUT = range(5)
 
 
+def total_of(terms):
+    while len(terms) > 1:
+        terms = [sum(terms[i + 1:i + 2], terms[i]) for i in range(0, len(terms), 2)]
+    return terms[0]
+
+
 def mixer_kernel(
-    pre_ref, post_ref, feat_ref, decay_ref, resid_ref, skip_ref, q_ref, k_ref,
+    pre_hbm, feat_hbm, decay_hbm, resid_hbm, skip_hbm, q_hbm, k_hbm, post_hbm,
     filt_ref, att_ref,
+    pre_ref, feat_ref, decay_ref, resid_ref, skip_ref, q_ref, k_ref, post_ref,
     qk_send, qk_all, st_send, st_all, pf_send, pf_all, v_send, v_all, att_send, att_all,
     driven, conv, factor, gain, state, jump, weights, totals,
-    send_sems, recv_sems,
+    send_sems, recv_sems, load_sems,
 ):
+    sources = (pre_hbm, feat_hbm, decay_hbm, resid_hbm, skip_hbm, q_hbm, k_hbm, post_hbm)
+    places = (pre_ref, feat_ref, decay_ref, resid_ref, skip_ref, q_ref, k_ref, post_ref)
+    loads = [
+        pltpu.make_async_copy(source, place, load_sems.at[i])
+        for i, (source, place) in enumerate(zip(sources, places))
+    ]
+    for load in loads:
+        load.start()
     heads, rows, size = v_send.shape
     modes = decay_ref.shape[0]
     me = lax.axis_index("ctx")
@@ -135,6 +150,8 @@
         dst[me] = src[me]
         return copies
 
+    for load in loads[:5]:
+        load.wait()
     for h in range(heads):
         lanes = slice(h * size, (h + 1) * size)
         product = pre_ref[:, lanes].astype(jnp.float32) * feat_ref[:, lanes].astype(jnp.float32)
@@ -165,11 +182,27 @@
 
     pl.semaphore_wait(barrier, heads - 1)
     st_copies = exchange(STATE, st_send, st_all)
+    for load in loads[5:]:
+        load.wait()
     for h in range(heads):
         lanes = slice(h * size, (h + 1) * size)
         qk_send[h, 0] = q_ref[:, lanes]
         qk_send[h, 1] = k_ref[:, lanes]
     qk_copies = exchange(QK, qk_send, qk_all)
+
+    g = by_mode(gain)
+    skip = skip_ref[...]
+
+    def filter_rows(turn, s):
+        for u in range(step):
+            at = pl.ds(turn * step + u, heads, stride=rows)
+            d = driven[at, :]
+            s = [f[m] * s[m] + d for m in range(modes)]
+            terms = [g[m] * s[m] for m in range(modes)] + [skip * d]
+            conv[at, :] = total_of(terms)
+        return s
+
+    lax.fori_loop(0, rows // step, filter_rows, zero)
 
     for copy in st_copies:
         copy.wait_recv()
@@ -184,21 +217,15 @@
     for h in range(heads):
         state[h * modes:(h + 1) * modes] = pf_all[h].astype(jnp.float32)
 
-    g = by_mode(gain)
-    skip = skip_ref[...]
-
-    def filter_rows(turn, s):
+    def add_incoming(turn, s):
         for u in range(step):
             at = pl.ds(turn * step + u, heads, stride=rows)
-            d = driven[at, :]
-            s = [f[m] * s[m] + d for m in range(modes)]
-            terms = [g[m] * s[m] for m in range(modes)] + [skip * d]
-            while len(terms) > 1:
-                terms = [sum(terms[i + 1:i + 2], terms[i]) for i in range(0, len(terms), 2)]
-            conv[at, :] = terms[0]
+            s = [f[m] * s[m] for m in range(modes)]
+            conv[at, :] += total_of(s)
         return s
 
-    lax.fori_loop(0, rows // step, filter_rows, by_mode(state))
+    start = [g[m] * s for m, s in enumerate(by_mode(state))]
+    lax.fori_loop(0, rows // step, add_incoming, start)
     for h in range(heads):
         lanes = slice(h * size, (h + 1) * size)
         gated = post_ref[:, lanes].astype(jnp.float32) * conv[h * rows:(h + 1) * rows]
@@ -261,9 +288,11 @@
     return tuple(pl.pallas_call(
         mixer_kernel,
         out_shape=(shape, shape),
-        in_specs=[pl.BlockSpec(memory_space=pltpu.VMEM)] * 8,
+        in_specs=[pl.BlockSpec(memory_space=pltpu.HBM)] * 8,
         out_specs=(pl.BlockSpec(memory_space=pltpu.VMEM),) * 2,
         scratch_shapes=[
+            bf16(rows, width), bf16(rows, width), f32(modes, width), f32(modes, width),
+            f32(heads, size), bf16(rows, width), bf16(rows, width), bf16(rows, width),
             bf16(heads, 2, rows, size), bf16(heads, 2, rows, size),
             *small, *blocks,
             f32(heads * rows, size), f32(heads * rows, size),
@@ -271,13 +300,14 @@
             bf16(heads * rows, heads * rows), f32(heads * rows, size),
             pltpu.SemaphoreType.DMA((5, heads)),
             pltpu.SemaphoreType.DMA((5, heads)),
+            pltpu.SemaphoreType.DMA((8,)),
         ],
         compiler_params=pltpu.CompilerParams(
-            collective_id=0, has_side_effects=True, vmem_limit_bytes=32 * 1024 * 1024
+            collective_id=0, has_side_effects=True, vmem_limit_bytes=60 * 1024 * 1024
         ),
     )(
-        pre_gate, post_gate, features, decay_rates, residues,
-        skip_gain.reshape(heads, size), queries, key_rows,
+        pre_gate, features, decay_rates, residues, skip_gain.reshape(heads, size),
+        queries, key_rows, post_gate,
     ))
 
 

time: 34.6 us -> 28.8 us (0.83)
  local copies, waits for them, and re-layouts: 8.19 us -> 2.26 us
  Pallas kernels: 25.4 us -> 25.8 us
    unnamed x18 -> x4, local copies, waits for them, and re-layouts: 8.19 us -> 2.26 us
    pallas_call x1, Pallas kernels: 25.4 us -> 25.8 us  [by_heads(): pl.pallas_call(mixer_kernel, out_shape=(shape, shape), in_specs=[pl.Block...]
where the time goes in v2:
time: 28.8 us; the launch traced here: 28.7 us
  Pallas kernels  25.8 us (90%)
  local copies, waits for them, and re-layouts  2.26 us (8%)
  between operations  0.65 us (2%)
    pallas_call x1, Pallas kernels, by_heads(): pl.pallas_call(mixer_kernel, out_shape=(shape, shape), in_specs=[pl.Block...  25.8 us
    unnamed x4, local copies, waits for them, and re-layouts  2.26 us

profile of v2, /device:TPU:0, one launch (start us, length us, event | category | flops | bytes accessed | tf_op | source)
XLA Modules:
  0.0 28.7 jit_solution(3481604533755463815)
XLA Ops:
  0.6 25.8 %shard_map.95 = (bf16[64,1024]{1,0:T(8,128)(2,1)}, bf16[64,1024]{1,0:T(8,128)(2,1)}) custom-call(bf16[64,1024]{1,0:T(8,128)(2,1)} %pre_hbm.1, bf16[64,1024]{1,0:T(8,128)(2,1)} %feat_hbm.1, f32[16,1024]{1,0:T(8,128)} %decay_hbm.1, f32[16,1024]{1,0:T(8,128)} %resid_hbm.1, f32[8,128]{1,0:T(8,128)} %bitcast.1, bf16[64,1024]{1,0:T(8,128)(2,1)} %q_hbm.1, ...), custom_call_target="tpu_custom_call" | custom-call | tf_op jit(solution)/shard_map/pallas_call | solution.py:288
  26.4 0.0 copy-start
  26.4 1.6 %copy.12 = bf16[64,1024]{1,0:T(8,128)(2,1)} copy(bf16[64,1024]{1,0:T(8,128)(2,1)} %get-tuple-element.4) | data formatting | bytes 262144
  28.0 0.0 copy-done
  28.0 0.7 %copy.13 = bf16[64,1024]{1,0:T(8,128)(2,1)} copy(bf16[64,1024]{1,0:T(8,128)(2,1)S(1)} %copy-done) | data formatting | bytes 262144
Async XLA Ops:
  26.4 1.6 %copy-start = (bf16[64,1024]{1,0:T(8,128)(2,1)S(1)}, bf16[64,1024]{1,0:T(8,128)(2,1)}, u32[]{:S(2)}) copy-start(bf16[64,1024]{1,0:T(8,128)(2,1)} %get-tuple-element.5) | copy-start | bytes 393220
